TPU v7x, 32 devices: a whole 2x2x4 slice. The times are simulated.
32 devices in a mesh: rep: 2 (over y), seq: 4 (over z), tp: 4 (over x, core).
Axes of the slice: x: 2, y: 2, z: 4, core: 2. Of those that a mesh axis runs over, the one named last changes fastest.
Arguments:
- queries: bfloat16 [2048, 8192], P(('rep', 'seq'), 'tp'), parts along dimension 0, may hold values from -9 to 9
- keys: bfloat16 [2048, 1024], P(('rep', 'seq'), 'tp'), parts along dimension 0, may hold values from -9 to 9
- values: bfloat16 [2048, 1024], P(('rep', 'seq'), 'tp'), parts along dimension 0, may hold values from -6 to 6
- segments: int32 [2048], P(('rep', 'seq')), parts along dimension 0, may hold values from 0 to 15, as said below
Outputs:
- attended: bfloat16 [2048, 8192], P(('rep', 'seq'), 'tp'), parts along dimension 0
There are 2 independent parts, one for each index of `rep`. A program takes and returns all parts, laid end to end along the dimension named above; each array names one. Nothing has to cross between parts.
Inputs may be any that keep to these rules, and one draw needn't show every extreme that they name: `segments`: segment numbers never fall and each of the 16 documents has at least one token; document 0 is the longest, its 640 tokens are the first ones of the sequence; document 1 follows with exactly 192 tokens; the others have at most 1024 - 640 tokens each.
All inputs are finite; a program needn't handle non-finite values.
Results may differ from a plain program's by a relative error of at most 0.0075.
Values may be sent and summed in bfloat16 or wider, within the bound.
A program may use at most 64 MiB of HBM per device.

v0:
```python
from functools import partial
import math

import jax
import jax.numpy as jnp
from jax import lax
from jax.sharding import PartitionSpec as P

HEAD_DIM = 128
DOCS = 16


def carried_in(part, axis, combine, identity):
    place = lax.axis_index(axis)
    gathered = lax.all_gather(part, axis)
    state = jnp.zeros_like(part) + jnp.asarray(identity, part.dtype)

    def one(step, state):
        return combine(state, lax.dynamic_index_in_dim(gathered, step, 0, False))

    return lax.fori_loop(0, place, one, state)


def rotate(rows_in, places, width):
    row_count = rows_in.shape[0]
    head_count = rows_in.shape[1] // width
    half_width = width // 2
    vectors = rows_in.astype(jnp.float32).reshape(row_count, head_count, width)
    frequency = 1000000.0 ** (-jnp.arange(half_width, dtype=jnp.float32) / half_width)
    angles = places.astype(jnp.float32)[:, None] * frequency[None, :]
    cos_part = jnp.cos(angles)[:, None, :]
    sin_part = jnp.sin(angles)[:, None, :]
    lower_half = vectors[..., :half_width]
    upper_half = vectors[..., half_width:]
    turned = jnp.concatenate(
        [
            lower_half * cos_part - upper_half * sin_part,
            upper_half * cos_part + lower_half * sin_part,
        ],
        axis=-1,
    )
    return turned.astype(jnp.bfloat16)


def shards(queries, keys, values, segments):
    local_rows = queries.shape[0]
    first_row = lax.axis_index("seq") * local_rows
    local_index = jnp.arange(local_rows, dtype=jnp.int32)
    member = (segments[:, None] == jnp.arange(DOCS, dtype=jnp.int32)[None, :]).astype(jnp.int32)
    counts = jnp.sum(member, axis=0)
    before = carried_in(
        counts, "seq", lambda earlier, later: earlier + later, jnp.zeros_like(counts)
    )
    running = jnp.cumsum(member, axis=0)
    places = jnp.sum(member * (before[None, :] + running - 1), axis=1)
    kv_local = keys.shape[1] // HEAD_DIM
    head_local = queries.shape[1] // HEAD_DIM
    group_size = head_local // kv_local
    scale_factor = 1.0 / math.sqrt(HEAD_DIM)
    query_rot = rotate(queries, places, HEAD_DIM)
    key_rot = rotate(keys, places, HEAD_DIM).reshape(local_rows, kv_local * HEAD_DIM)
    kv_own = jnp.stack((key_rot, values), axis=1)
    seg_own = segments.astype(jnp.bfloat16)
    query_rows, query_segs = (query_rot, seg_own)
    query_index = first_row + local_index
    query_heads = jnp.transpose(
        query_rows.reshape(local_rows, kv_local, group_size, HEAD_DIM), (1, 2, 0, 3)
    )
    seg_rows = query_segs.astype(jnp.float32)
    block_count = 4
    block_rows = local_rows // block_count

    def absorb(carried, fragment, offset, lower):
        upper = lower + block_rows
        running_max, running_sum, accumulated = carried
        kv_frag, seg_frag = fragment
        span = kv_frag.shape[0]
        block_heads = query_heads[:, :, lower:upper]
        block_index = query_index[lower:upper]
        block_seg = seg_rows[lower:upper]
        key_heads = jnp.transpose(kv_frag[:, 0].reshape(span, kv_local, HEAD_DIM), (1, 0, 2))
        value_heads = jnp.transpose(kv_frag[:, 1].reshape(span, kv_local, HEAD_DIM), (1, 0, 2))
        key_index = jnp.arange(span, dtype=jnp.int32)
        allowed = (key_index[None, :] <= block_index[:, None]) & (key_index[None, :] >= 0)
        allowed = allowed & (seg_frag.astype(jnp.float32)[None, :] == block_seg[:, None])
        scores = (
            jnp.einsum("kgqd,kpd->kgqp", block_heads, key_heads, preferred_element_type=jnp.float32)
            * scale_factor
        )
        scores = jnp.where(allowed[None, None], scores, -1e30)
        new_max = jnp.maximum(running_max, jnp.max(scores, axis=-1))
        weights = jnp.where(allowed[None, None], jnp.exp(scores - new_max[..., None]), 0.0)
        new_sum = jnp.sum(weights, axis=-1)
        mixed = jnp.einsum(
            "kgqp,kpd->kgqd",
            weights.astype(jnp.bfloat16),
            value_heads,
            preferred_element_type=jnp.float32,
        )
        return (new_max, new_sum, mixed)

    initial = (
        jnp.full((kv_local, group_size, local_rows), -1e30, jnp.float32),
        jnp.zeros((kv_local, group_size, local_rows), jnp.float32),
        jnp.zeros((kv_local, group_size, local_rows, HEAD_DIM), jnp.float32),
    )
    fragment = (
        lax.all_gather(kv_own, "seq", axis=0, tiled=True),
        lax.all_gather(seg_own, "seq", axis=0, tiled=True),
    )
    offset = jnp.int32(0)
    kv_frag, seg_frag = fragment
    span = kv_frag.shape[0]
    outcomes = []
    for block_id in range(block_count):
        lower = block_id * block_rows
        upper = lower + block_rows
        state = tuple((member_state[:, :, lower:upper] for member_state in initial))
        useful = (offset <= query_index[upper - 1]) & (offset + span > 0)
        updated = lax.cond(
            useful,
            partial(absorb, fragment=fragment, offset=offset, lower=lower),
            lambda kept: kept,
            state,
        )
        outcomes.append(updated)
    carried = tuple(
        (
            jnp.concatenate([found[member_id] for found in outcomes], axis=2)
            for member_id in range(3)
        )
    )
    running_max, running_sum, accumulated = carried
    outcome = accumulated / running_sum[..., None]
    outcome = jnp.transpose(outcome, (2, 0, 1, 3)).reshape(local_rows, head_local * HEAD_DIM)
    outcome = outcome.astype(jnp.bfloat16)
    return outcome


def solution(mesh):
    placed = (
        P(("rep", "seq"), "tp"),
        P(("rep", "seq"), "tp"),
        P(("rep", "seq"), "tp"),
        P(("rep", "seq")),
    )
    return jax.shard_map(
        shards, mesh=mesh, in_specs=placed, out_specs=P(("rep", "seq"), "tp"), check_vma=False
    )
```

profile of v0, /device:TPU:0, one launch (start us, length us, event | category | flops | bytes accessed | tf_op | source)
XLA Modules:
  0.0 90.2 jit_solution(7919798758949753585)
XLA Ops:
  7.4 1.3 %dynamic-slice = u32[1]{0:T(128)} dynamic-slice(u32[32]{0:T(128)} %constant.93, u32[]{:T(128)S(6)} %add.39), dynamic_slice_sizes={1} | dynamic-slice | bytes 12
  9.6 9.9 %all-reduce = s32[64]{0:T(128)S(1)} all-reduce(s32[64]{0:T(128)S(1)} %dynamic-update-slice), channel_id=2, replica_groups=mesh['rep'=2,'seq'=4,'tp'=4] {'seq'}, use_global_device_ids=true, to_apply=%add | all-reduce | flops 64 | bytes 512
  21.9 1.0 %copy.38 = bf16[256,1,256]{0,2,1:T(8,128)(2,1)S(1)} copy(bf16[256,1,256]{2,0,1:T(8,128)(2,1)} %bitcast.134) | data formatting | bytes 262144 | tf_op jit(solution)/shard_map/stack | solution.py:62
  22.9 1.0 %copy.37 = f32[256,256]{0,1:T(8,128)S(1)} copy(bf16[256,256]{1,0:T(8,128)(2,1)} %param.15) | data formatting | bytes 393216 | tf_op jit(solution)/shard_map/reshape | solution.py:28
  29.1 9.2 %all-gather.1 = bf16[4,1,256]{2,1,0:T(2,128)(2,1)S(1)} all-gather(bf16[1,1,256]{2,1,0:T(2,128)(2,1)S(1)} %reshape.345), channel_id=1, replica_groups=mesh['rep'=2,'seq'=4,'tp'=4] {'seq'}, dimensions={0}, use_global_device_ids=true | all-gather | bytes 2560 | tf_op jit(solution)/shard_map/all_gather | solution.py:109
  38.4 1.5 %convert_bitcast_fusion = f32[32,8,16,128]{3,1,2,0:T(8,128)S(1)} fusion(bf16[256,2048]{1,0:T(8,128)(2,1)} %param.14), kind=kLoop, calls=%fused_computation.71 | loop fusion | flops 524288 | bytes 3145728
  40.9 1.4 %subtract_convert_fusion = (bf16[256,16,64]{2,0,1:T(8,128)(2,1)S(1)}, bf16[256,16,64]{2,0,1:T(8,128)(2,1)S(1)}) fusion(f32[256,16,64]{2,1,0:T(8,128)S(1)} %get-tuple-element.134, f32[256,16,64]{2,1,0:T(8,128)S(1)} %get-tuple-element.133, f32[256,64]{1,0:T(8,128)S(1)} %copy.36, f32[256,64]{1,0:T(8,128)S(1)} %copy.34), kind=kLoop, calls=%fused_computation.73 | loop fusion | flops 2097152 | bytes 3276800 | tf_op jit(solution)/shard_map/convert.11
  42.9 11.7 %all-gather.4.cloned.1.call-done = bf16[1024,2,256]{0,2,1:T(8,128)(2,1)} async-done(((bf16[256,2,256]{0,2,1:T(8,128)(2,1)}), bf16[1024,2,256]{0,2,1:T(8,128)(2,1)}) %all-gather.4.cloned.1.call-update) | async-done | bytes 1048592 | tf_op jit(solution)/shard_map/all_gather | solution.py:108
  54.6 5.4 %conditional.7 = (f32[2,8,64]{2,1,0:T(8,128)S(1)}, f32[2,8,64,128]{3,2,1,0:T(8,128)S(1)}) conditional(s32[]{:T(128)} %bitcast.45, () %tuple.46, (s32[256]{0:T(256)S(1)}, bf16[1024]{0:T(1024)(128)(2,1)S(1)}, f32[256]{0:T(256)S(1)}, bf16[2,8,256,128]{3,2,1,0:T(8,128)(2,1)S(1)}, bf16[1024,2,256]{0,2,1:T(8,128)(2,1)}) %tuple.84), branch_computations={%region_18.19_spmd, %region_19.22_spmd} | conditional | flops 550699008 | bytes 18910736 | solution.py:120
  54.9 1.3 %fusion.67 = (bf16[1024,1,256]{0,2,1:T(8,128)(2,1)S(1)}, bf16[1024,1,256]{0,2,1:T(8,128)(2,1)S(1)}) fusion(bf16[1024,2,256]{0,2,1:T(8,128)(2,1)} %get-tuple-element.86), kind=kLoop, calls=%fused_computation.101 | loop fusion | bytes 2097152 | tf_op jit(solution)/shard_map/cond/branch_1_fun/slice | solution.py:82
  56.7 0.9 fusion.42
  57.6 1.1 %fusion.45 = f32[2,8,64,128]{3,2,1,0:T(8,128)S(1)} fusion(f32[2,8,64,1024]{3,2,1,0:T(8,128)S(1)} %get-tuple-element.130, f32[2,8,64]{2,1,0:T(8,128)S(1)} %broadcast_maximum_fusion.3, pred[64,1024]{1,0:T(8,128)(4,1)S(1)} %fusion.52, bf16[1024,2,128]{2,0,1:T(8,128)(2,1)S(1)} %copy.31), kind=kOutput, calls=%fused_computation.57 | convolution fusion | flops 273678336 | bytes 5312512 | tf_op jit(solution)/shard_map/cond/branch_1_fun/kgqp,kpd->kgqd/dot_general | solution.py:94
  58.7 1.3 %fusion.44 = f32[2,8,64]{2,1,0:T(8,128)S(1)} fusion(f32[2,8,64,1024]{3,2,1,0:T(8,128)S(1)} %get-tuple-element.130, f32[2,8,64]{2,1,0:T(8,128)S(1)} %broadcast_maximum_fusion.3, pred[64,1024]{1,0:T(8,128)(4,1)S(1)} %fusion.52), kind=kLoop, calls=%fused_computation.56 | loop fusion | flops 5241856 | bytes 4268032 | tf_op jit(solution)/shard_map/cond/branch_1_fun/reduce_sum | solution.py:93
  60.0 5.5 %conditional.6 = (f32[2,8,64]{2,1,0:T(8,128)S(1)}, f32[2,8,64,128]{3,2,1,0:T(8,128)S(1)}) conditional(s32[]{:T(128)} %bitcast.44, () %tuple.45, (s32[256]{0:T(256)S(1)}, bf16[1024]{0:T(1024)(128)(2,1)S(1)}, f32[256]{0:T(256)S(1)}, bf16[2,8,256,128]{3,2,1,0:T(8,128)(2,1)S(1)}, bf16[1024,2,256]{0,2,1:T(8,128)(2,1)}) %tuple.85), branch_computations={%region_14.15_spmd, %region_15.18_spmd} | conditional | flops 550699008 | bytes 18910736 | solution.py:120
  60.4 1.3 %fusion.66 = (bf16[1024,1,256]{0,2,1:T(8,128)(2,1)S(1)}, bf16[1024,1,256]{0,2,1:T(8,128)(2,1)S(1)}) fusion(bf16[1024,2,256]{0,2,1:T(8,128)(2,1)} %get-tuple-element.81), kind=kLoop, calls=%fused_computation.100 | loop fusion | bytes 2097152 | tf_op jit(solution)/shard_map/cond/branch_1_fun/slice | solution.py:82
  62.2 0.9 fusion.28
  63.1 1.1 %fusion.31 = f32[2,8,64,128]{3,2,1,0:T(8,128)S(1)} fusion(f32[2,8,64,1024]{3,2,1,0:T(8,128)S(1)} %get-tuple-element.126, f32[2,8,64]{2,1,0:T(8,128)S(1)} %broadcast_maximum_fusion.2, pred[64,1024]{1,0:T(8,128)(4,1)S(1)} %fusion.38, bf16[1024,2,128]{2,0,1:T(8,128)(2,1)S(1)} %copy.29), kind=kOutput, calls=%fused_computation.40 | convolution fusion | flops 273678336 | bytes 5312512 | tf_op jit(solution)/shard_map/cond/branch_1_fun/kgqp,kpd->kgqd/dot_general | solution.py:94
  64.2 1.3 %fusion.30 = f32[2,8,64]{2,1,0:T(8,128)S(1)} fusion(f32[2,8,64,1024]{3,2,1,0:T(8,128)S(1)} %get-tuple-element.126, f32[2,8,64]{2,1,0:T(8,128)S(1)} %broadcast_maximum_fusion.2, pred[64,1024]{1,0:T(8,128)(4,1)S(1)} %fusion.38), kind=kLoop, calls=%fused_computation.39 | loop fusion | flops 5241856 | bytes 4268032 | tf_op jit(solution)/shard_map/cond/branch_1_fun/reduce_sum | solution.py:93
  65.5 7.1 %conditional.5 = (f32[2,8,64]{2,1,0:T(8,128)S(1)}, f32[2,8,64,128]{3,2,1,0:T(8,128)}) conditional(s32[]{:T(128)} %bitcast.43, () %tuple.44, (s32[256]{0:T(256)S(1)}, bf16[1024]{0:T(1024)(128)(2,1)S(1)}, f32[256]{0:T(256)S(1)}, bf16[2,8,256,128]{3,2,1,0:T(8,128)(2,1)S(1)}, bf16[1024,2,256]{0,2,1:T(8,128)(2,1)}) %tuple.86), branch_computations={%region_10.11_spmd, %region_11.14_spmd} | conditional | flops 550699008 | bytes 21007916 | solution.py:120
  65.8 1.3 %fusion.65 = (bf16[1024,1,256]{0,2,1:T(8,128)(2,1)S(1)}, bf16[1024,1,256]{0,2,1:T(8,128)(2,1)S(1)}) fusion(bf16[1024,2,256]{0,2,1:T(8,128)(2,1)} %get-tuple-element.76), kind=kLoop, calls=%fused_computation.99 | loop fusion | bytes 2097152 | tf_op jit(solution)/shard_map/cond/branch_1_fun/slice | solution.py:82
  67.1 1.0 %copy.27 = bf16[1024,2,128]{2,0,1:T(8,128)(2,1)} copy(bf16[1024,2,128]{0,2,1:T(8,128)(2,1)S(1)} %bitcast.130) | data formatting | bytes 1048576 | tf_op jit(solution)/shard_map/cond/branch_1_fun/reshape;cond/branch_1_fun/squeeze | solution.py:82
  68.4 0.9 fusion.14
  69.4 1.9 %fusion.17 = f32[2,8,64,128]{3,2,1,0:T(8,128)} fusion(f32[2,8,64,1024]{3,2,1,0:T(8,128)S(1)} %get-tuple-element.122, f32[2,8,64]{2,1,0:T(8,128)S(1)} %broadcast_maximum_fusion.1, pred[64,1024]{1,0:T(8,128)(4,1)S(1)} %fusion.24, bf16[1024,2,128]{2,0,1:T(8,128)(2,1)S(1)} %copy-done.1), kind=kOutput, calls=%fused_computation.23 | convolution fusion | flops 273678336 | bytes 5312512 | tf_op jit(solution)/shard_map/cond/branch_1_fun/kgqp,kpd->kgqd/dot_general | solution.py:94
  71.3 1.3 %fusion.16 = f32[2,8,64]{2,1,0:T(8,128)S(1)} fusion(f32[2,8,64,1024]{3,2,1,0:T(8,128)S(1)} %get-tuple-element.122, f32[2,8,64]{2,1,0:T(8,128)S(1)} %broadcast_maximum_fusion.1, pred[64,1024]{1,0:T(8,128)(4,1)S(1)} %fusion.24), kind=kLoop, calls=%fused_computation.22 | loop fusion | flops 5241856 | bytes 4268032 | tf_op jit(solution)/shard_map/cond/branch_1_fun/reduce_sum | solution.py:93
  72.6 6.2 %conditional.4 = (f32[2,8,64]{2,1,0:T(8,128)S(1)}, f32[2,8,64,128]{3,2,1,0:T(8,128)S(1)}) conditional(s32[]{:T(128)} %bitcast.33, () %tuple.41, (s32[256]{0:T(256)S(1)}, bf16[1024]{0:T(1024)(128)(2,1)S(1)}, f32[256]{0:T(256)S(1)}, bf16[2,8,256,128]{3,2,1,0:T(8,128)(2,1)S(1)}, bf16[1024,2,256]{0,2,1:T(8,128)(2,1)}) %tuple.87), branch_computations={%region_6.7_spmd, %region_7.10_spmd} | conditional | flops 550699008 | bytes 21007916 | solution.py:120
  72.8 1.3 %fusion.64 = (bf16[1024,1,256]{0,2,1:T(8,128)(2,1)S(1)}, bf16[1024,1,256]{0,2,1:T(8,128)(2,1)S(1)}) fusion(bf16[1024,2,256]{0,2,1:T(8,128)(2,1)} %get-tuple-element.71), kind=kLoop, calls=%fused_computation.98 | loop fusion | bytes 2097152 | tf_op jit(solution)/shard_map/cond/branch_1_fun/slice | solution.py:82
  74.1 1.0 %copy.25 = bf16[1024,2,128]{2,0,1:T(8,128)(2,1)} copy(bf16[1024,2,128]{0,2,1:T(8,128)(2,1)S(1)} %bitcast.131) | data formatting | bytes 1048576 | tf_op jit(solution)/shard_map/cond/branch_1_fun/reshape;cond/branch_1_fun/squeeze | solution.py:82
  75.4 0.9 fusion
  76.4 1.1 %fusion.3 = f32[2,8,64,128]{3,2,1,0:T(8,128)S(1)} fusion(f32[2,8,64,1024]{3,2,1,0:T(8,128)S(1)} %get-tuple-element.118, f32[2,8,64]{2,1,0:T(8,128)S(1)} %broadcast_maximum_fusion, pred[64,1024]{1,0:T(8,128)(4,1)S(1)} %fusion.10, bf16[1024,2,128]{2,0,1:T(8,128)(2,1)S(1)} %copy-done.2), kind=kOutput, calls=%fused_computation.6 | convolution fusion | flops 273678336 | bytes 5312512 | tf_op jit(solution)/shard_map/cond/branch_1_fun/kgqp,kpd->kgqd/dot_general | solution.py:94
  77.5 1.3 %fusion.2 = f32[2,8,64]{2,1,0:T(8,128)S(1)} fusion(f32[2,8,64,1024]{3,2,1,0:T(8,128)S(1)} %get-tuple-element.118, f32[2,8,64]{2,1,0:T(8,128)S(1)} %broadcast_maximum_fusion, pred[64,1024]{1,0:T(8,128)(4,1)S(1)} %fusion.10), kind=kLoop, calls=%fused_computation.5 | loop fusion | flops 5241856 | bytes 4268032 | tf_op jit(solution)/shard_map/cond/branch_1_fun/reduce_sum | solution.py:93
  79.7 1.8 %fusion.57 = bf16[256,2,8,128]{3,0,2,1:T(8,128)(2,1)S(1)} fusion(f32[2,8,256]{2,1,0:T(8,128)S(1)} %pad_maximum_fusion.2, f32[2,8,64,128]{3,2,1,0:T(8,128)S(1)} %get-tuple-element.100, f32[2,8,64,128]{3,2,1,0:T(8,128)S(1)} %get-tuple-element.99, f32[2,8,64,128]{3,2,1,0:T(8,128)} %get-tuple-element.98, f32[2,8,64,128]{3,2,1,0:T(8,128)} %copy-done), kind=kLoop, calls=%fused_computation.76 | loop fusion | flops 2621440 | bytes 3162112 | tf_op jit(solution)/shard_map/convert_element_type | solution.py:136
  82.1 1.2 %copy.60 = bf16[32,8,16,128]{3,1,2,0:T(8,128)(2,1)} copy(bf16[32,8,16,128]{3,2,1,0:T(8,128)(2,1)S(1)} %bitcast.123) | data formatting | bytes 2097152
  (65 shorter events, 12.0 us)
Async XLA Ops:
  6.5 48.1 %all-gather.4.cloned.1.call-start = ((), (), s32[]{:S(2)}) async-start(), calls=%async_computation | async-start | bytes 1310720 | tf_op jit(solution)/shard_map/all_gather | solution.py:108
  68.4 1.0 %copy-start.1 = (bf16[1024,2,128]{2,0,1:T(8,128)(2,1)S(1)}, bf16[1024,2,128]{2,0,1:T(8,128)(2,1)}, u32[]{:S(2)}) copy-start(bf16[1024,2,128]{2,0,1:T(8,128)(2,1)} %copy.27) | copy-start | bytes 1572868 | tf_op jit(solution)/shard_map/cond
  75.4 1.0 %copy-start.2 = (bf16[1024,2,128]{2,0,1:T(8,128)(2,1)S(1)}, bf16[1024,2,128]{2,0,1:T(8,128)(2,1)}, u32[]{:S(2)}) copy-start(bf16[1024,2,128]{2,0,1:T(8,128)(2,1)} %copy.25) | copy-start | bytes 1572868 | tf_op jit(solution)/shard_map/cond
  78.9 0.8 copy-start
Sparse Core Ops, SparseCore 0:
  25.1 29.4 all-gather.3
where the time goes:
time: 90.7 us; the launch traced here: 90.2 us
  blocking collectives  19.1 us (21%)
  local copies, waits for them, and re-layouts  17.8 us (20%)
  between operations  16.7 us (18%)
  other arithmetic  15.8 us (17%)
  waiting for transfers between devices  11.7 us (13%)
  matrix products  8.54 us (9%)
    all_gather x1, waiting for transfers between devices, shards(): lax.all_gather(kv_own, 'seq', axis=0, tiled=True)  11.7 us
    unnamed x1, blocking collectives  9.89 us
    all_gather x1, blocking collectives, shards(): lax.all_gather(seg_own, 'seq', axis=0, tiled=True)  9.24 us
    reduce_sum x4, other arithmetic, absorb(): new_sum = jnp.sum(weights, axis=-1)  5.37 us
    slice x4, local copies, waits for them, and re-layouts, absorb(): kv_frag[:, 1].reshape(span, kv_local, HEAD_DIM)  5.08 us
    dot_general x4, matrix products, absorb(): jnp.einsum('kgqp,kpd->kgqd', weights.astype(jnp.bfloat16), value_heads, p...  5.06 us
    unnamed x9, local copies, waits for them, and re-layouts  3.92 us
    dot_general x4, matrix products, absorb(): jnp.einsum('kgqd,kpd->kgqp', block_heads, key_heads, preferred_element_ty...  3.48 us
  transfers between devices with their start and end apart: 1, of which 1 were waited for; matrix products, arithmetic and copies ran while one was open for 7% of the time, Pallas kernels for 0%

commit v1 on v0

v1 whole, which is shorter than its diff:
```python
import functools
import math

import jax
import jax.numpy as jnp
from jax import lax
from jax.experimental import pallas as pl
from jax.experimental.pallas import tpu as pltpu
from jax.sharding import PartitionSpec as P

HEAD_DIM = 128
HALF = 128
SECOND_DOC = 192
MASKED = -1e30
EXPONENT = math.log2(math.e) / math.sqrt(HEAD_DIM)
MESH = pl.DeviceIdType.MESH


def first_key_block(tile, doc0):
    later = jnp.where(tile < (doc0 + SECOND_DOC) // HALF + 1, doc0 // HALF, (doc0 + SECOND_DOC) // HALF)
    return jnp.where(tile < doc0 // HALF, 0, later)


def kernel(
    n, doc0, has_before, q_ref, k_ref, v_ref, seg_ref, *refs
):
    before_ref = refs[0] if has_before else None
    (
    out_ref, k_all, v_all, q_rot, acc, top, total, cos_ref, sin_ref, start_ref,
    send_sem, recv_sem, own_sem,
    ) = refs[has_before:]
    me = lax.axis_index("seq")
    rows = k_ref.shape[0]
    halves = rows // HALF
    kv_heads = k_ref.shape[1] // HEAD_DIM
    group = q_ref.shape[1] // k_ref.shape[1]
    first_row = me * rows

    barrier = pltpu.get_barrier_semaphore()
    for step in range(1, n):
        pl.semaphore_signal(
            barrier, inc=1, device_id={"seq": lax.rem(me + step, n)}, device_id_type=MESH
        )

    def first_source(device):
        low = first_key_block(device * halves, doc0)
        for half in range(1, halves):
            low = jnp.minimum(low, first_key_block(device * halves + half, doc0))
        return low // halves

    def wanted(step):
        other = me + step
        return (other < n) & (me >= first_source(other))

    def send(step, kind):
        source = v_ref if kind else k_all.at[me]
        target = v_all.at[me] if kind else k_all.at[me]
        return pltpu.make_async_remote_copy(
            src_ref=source,
            dst_ref=target,
            send_sem=send_sem.at[step, kind],
            recv_sem=recv_sem.at[step, kind],
            device_id={"seq": lax.rem(me + step, n)},
            device_id_type=MESH,
        )

    own_v = pltpu.make_async_copy(v_ref, v_all.at[me], own_sem)
    own_v.start()
    pl.semaphore_wait(barrier, n - 1)

    for step in range(1, n):
        @pl.when(wanted(step))
        def _():
            send(step, 1).start()

    seg_row = jnp.broadcast_to(seg_ref[...], (rows, rows))
    earlier = (seg_row < seg_row.T).astype(jnp.float32)
    local_before = jnp.sum(earlier, axis=1, keepdims=True).astype(jnp.int32)
    token = first_row + lax.broadcasted_iota(jnp.int32, (rows, 1), 0)
    start = first_row + local_before
    if has_before:
        start = jnp.where(local_before == 0, before_ref[0, 0], start)
    start = jnp.where(token < doc0, 0, jnp.where(token < doc0 + SECOND_DOC, doc0, start))
    start_ref[...] = start
    lane = lax.broadcasted_iota(jnp.int32, (1, HEAD_DIM), 1)
    index = (lane % (HEAD_DIM // 2)).astype(jnp.float32)
    frequency = jnp.exp(index * (-math.log(1000000.0) / (HEAD_DIM // 2)))
    angles = (token - start).astype(jnp.float32) * frequency
    cos_ref[...] = jnp.cos(angles)
    sin_ref[...] = jnp.where(lane < HEAD_DIM // 2, -1.0, 1.0) * jnp.sin(angles)

    def turn(x, cos_part, sin_part):
        wide = x.astype(jnp.float32)
        swapped = pltpu.roll(wide, HEAD_DIM // 2, 1)
        return (wide * cos_part + swapped * sin_part).astype(jnp.bfloat16)

    for head in range(kv_heads):
        columns = slice(head * HEAD_DIM, (head + 1) * HEAD_DIM)
        k_all[me, :, columns] = turn(k_ref[:, columns], cos_ref[...], sin_ref[...])
    for step in range(1, n):
        @pl.when(wanted(step))
        def _():
            send(step, 0).start()

    for half in range(halves):
        part = slice(half * HALF, (half + 1) * HALF)
        for head in range(kv_heads * group):
            columns = slice(head * HEAD_DIM, (head + 1) * HEAD_DIM)
            q_rot[half, head] = turn(q_ref[part, columns], cos_ref[part], sin_ref[part])

    def scores(half, kv, head, source, upto, allowed):
        columns = slice(kv * HEAD_DIM, (kv + 1) * HEAD_DIM)
        found = lax.dot_general(
            q_rot[half, head],
            k_all[source, :upto, columns],
            (((1,), (1,)), ((), ())),
            preferred_element_type=jnp.float32,
        )
        return jnp.where(allowed, found, MASKED)

    def mask(half, source, upto):
        part = slice(half * HALF, (half + 1) * HALF)
        key = source * rows + lax.broadcasted_iota(jnp.int32, (1, upto), 1)
        query = first_row + half * HALF + lax.broadcasted_iota(jnp.int32, (HALF, 1), 0)
        return (key >= start_ref[part]) & (key <= query)

    own_v.wait()
    for half in range(halves):
        upto = (half + 1) * HALF
        allowed = mask(half, me, upto)
        for head in range(kv_heads * group):
            kv = head // group
            columns = slice(kv * HEAD_DIM, (kv + 1) * HEAD_DIM)
            found = scores(half, kv, head, me, upto, allowed)
            peak = jnp.max(found, axis=1, keepdims=True)
            weight = jnp.exp2((found - peak) * EXPONENT)
            top[half, head] = peak
            total[half, head] = jnp.sum(weight, axis=1, keepdims=True)
            acc[half, head] = jnp.dot(
                weight.astype(jnp.bfloat16),
                v_all[me, :upto, columns],
                preferred_element_type=jnp.float32,
            )

    def absorb(step, carry):
        source = me - step
        arrived = pltpu.make_async_remote_copy(
            src_ref=k_all.at[source], dst_ref=k_all.at[source],
            send_sem=send_sem.at[step, 0], recv_sem=recv_sem.at[step, 0],
            device_id={"seq": lax.rem(me + step, n)}, device_id_type=MESH,
        )
        arrived.wait_recv()
        arrived = pltpu.make_async_remote_copy(
            src_ref=v_all.at[source], dst_ref=v_all.at[source],
            send_sem=send_sem.at[step, 1], recv_sem=recv_sem.at[step, 1],
            device_id={"seq": lax.rem(me + step, n)}, device_id_type=MESH,
        )
        arrived.wait_recv()
        for half in range(halves):
            low = first_key_block(me * halves + half, doc0)

            @pl.when((source + 1) * halves > low)
            def _():
                allowed = mask(half, source, rows)
                for head in range(kv_heads * group):
                    kv = head // group
                    columns = slice(kv * HEAD_DIM, (kv + 1) * HEAD_DIM)
                    found = scores(half, kv, head, source, rows, allowed)
                    old = top[half, head]
                    peak = jnp.maximum(old, jnp.max(found, axis=1, keepdims=True))
                    weight = jnp.exp2((found - peak) * EXPONENT)
                    shrink = jnp.exp2((old - peak) * EXPONENT)
                    top[half, head] = peak
                    total[half, head] = total[half, head] * shrink + jnp.sum(
                        weight, axis=1, keepdims=True
                    )
                    acc[half, head] = acc[half, head] * shrink + jnp.dot(
                        weight.astype(jnp.bfloat16),
                        v_all[source, :, columns],
                        preferred_element_type=jnp.float32,
                    )
        return carry

    lax.fori_loop(1, me - first_source(me) + 1, absorb, 0)

    for half in range(halves):
        part = slice(half * HALF, (half + 1) * HALF)
        for head in range(kv_heads * group):
            columns = slice(head * HEAD_DIM, (head + 1) * HEAD_DIM)
            out_ref[part, columns] = (acc[half, head] / total[half, head]).astype(jnp.bfloat16)

    for step in range(1, n):
        @pl.when(wanted(step))
        def _():
            send(step, 1).wait_send()
            send(step, 0).wait_send()


def shards(n, queries, keys, values, segments):
    rows = queries.shape[0]
    tokens = n * rows
    doc0 = tokens // 2 + HALF
    kv_heads = keys.shape[1] // HEAD_DIM
    heads = queries.shape[1] // HEAD_DIM
    halves = rows // HALF
    operands = [queries, keys, values, segments.reshape(1, rows)]
    specs = [pl.BlockSpec(memory_space=pltpu.VMEM)] * 4
    has_before = (doc0 + SECOND_DOC) // rows < n - 1
    if has_before:
        every = lax.all_gather(segments, "seq", axis=0, tiled=True)
        before = jnp.sum((every < segments[0]).astype(jnp.int32))
        operands.append(before.reshape(1, 1))
        specs.append(pl.BlockSpec(memory_space=pltpu.SMEM))
    return pl.pallas_call(
        functools.partial(kernel, n, doc0, has_before),
        out_shape=jax.ShapeDtypeStruct(queries.shape, jnp.bfloat16),
        in_specs=specs,
        out_specs=pl.BlockSpec(memory_space=pltpu.VMEM),
        scratch_shapes=[
            pltpu.VMEM((n, rows, kv_heads * HEAD_DIM), jnp.bfloat16),
            pltpu.VMEM((n, rows, kv_heads * HEAD_DIM), jnp.bfloat16),
            pltpu.VMEM((halves, heads, HALF, HEAD_DIM), jnp.bfloat16),
            pltpu.VMEM((halves, heads, HALF, HEAD_DIM), jnp.float32),
            pltpu.VMEM((halves, heads, HALF, 1), jnp.float32),
            pltpu.VMEM((halves, heads, HALF, 1), jnp.float32),
            pltpu.VMEM((rows, HEAD_DIM), jnp.float32),
            pltpu.VMEM((rows, HEAD_DIM), jnp.float32),
            pltpu.VMEM((rows, 1), jnp.int32),
            pltpu.SemaphoreType.DMA((n, 2)),
            pltpu.SemaphoreType.DMA((n, 2)),
            pltpu.SemaphoreType.DMA,
        ],
        compiler_params=pltpu.CompilerParams(
            collective_id=0, has_side_effects=True, vmem_limit_bytes=48 * 1024 * 1024
        ),
    )(*operands)


def solution(mesh):
    placed = (
        P(("rep", "seq"), "tp"),
        P(("rep", "seq"), "tp"),
        P(("rep", "seq"), "tp"),
        P(("rep", "seq")),
    )
    return jax.shard_map(
        functools.partial(shards, mesh.shape["seq"]),
        mesh=mesh,
        in_specs=placed,
        out_specs=P(("rep", "seq"), "tp"),
        check_vma=False,
    )
```

time: 90.7 us -> 27.1 us (0.30)
  the two profiles are of different devices: /device:TPU:0 before, /device:TPU:8 now
where the time goes in v1:
time: 27.1 us; the launch traced here: 26.9 us
  Pallas kernels  22.2 us (82%)
  local copies, waits for them, and re-layouts  4.68 us (17%)
    pallas_call x1, Pallas kernels, shards(): pl.pallas_call(functools.partial(kernel, n, doc0, has_before), out_shape=...  22.2 us
    unnamed x9, local copies, waits for them, and re-layouts  4.68 us

profile of v1, /device:TPU:8, one launch (start us, length us, event | category | flops | bytes accessed | tf_op | source)
XLA Modules:
  0.0 26.9 jit_solution(17522011935723218084)
XLA Ops:
  0.0 0.0 copy-start.3
  0.0 0.7 %copy-done.3 = s32[256]{0:T(256)S(1)} copy-done((s32[256]{0:T(256)S(1)}, s32[256]{0:T(256)}, u32[]{:S(2)}) %copy-start.3) | copy-done | bytes 1048
  0.7 0.0 copy-start
  0.7 1.2 %copy-done = bf16[256,2048]{1,0:T(8,128)(2,1)S(1)} copy-done((bf16[256,2048]{1,0:T(8,128)(2,1)S(1)}, bf16[256,2048]{1,0:T(8,128)(2,1)}, u32[]{:S(2)}) %copy-start) | copy-done | bytes 1048600
  1.9 0.0 copy-start.1
  1.9 0.9 %copy-done.1 = bf16[256,256]{1,0:T(8,128)(2,1)S(1)} copy-done((bf16[256,256]{1,0:T(8,128)(2,1)S(1)}, bf16[256,256]{1,0:T(8,128)(2,1)}, u32[]{:S(2)}) %copy-start.1) | copy-done | bytes 131096
  2.8 0.0 copy-start.2
  2.8 0.9 %copy-done.2 = bf16[256,256]{1,0:T(8,128)(2,1)S(1)} copy-done((bf16[256,256]{1,0:T(8,128)(2,1)S(1)}, bf16[256,256]{1,0:T(8,128)(2,1)}, u32[]{:S(2)}) %copy-start.2) | copy-done | bytes 131096
  3.7 22.2 %shard_map.46 = bf16[256,2048]{1,0:T(8,128)(2,1)S(1)} custom-call(bf16[256,2048]{1,0:T(8,128)(2,1)S(1)} %copy-done, bf16[256,256]{1,0:T(8,128)(2,1)S(1)} %copy-done.1, bf16[256,256]{1,0:T(8,128)(2,1)S(1)} %copy-done.2, s32[1,256]{1,0:T(1,128)S(1)} %bitcast.1), custom_call_target="tpu_custom_call" | custom-call | tf_op jit(solution)/shard_map/pallas_call | solution.py:214
  25.9 1.0 %copy.6 = bf16[256,2048]{1,0:T(8,128)(2,1)} copy(bf16[256,2048]{1,0:T(8,128)(2,1)S(1)} %shard_map.46) | data formatting | bytes 2097152
Async XLA Ops:
  0.0 0.7 %copy-start.3 = (s32[256]{0:T(256)S(1)}, s32[256]{0:T(256)}, u32[]{:S(2)}) copy-start(s32[256]{0:T(256)} %param.7) | copy-start | bytes 3076
  0.7 1.2 %copy-start = (bf16[256,2048]{1,0:T(8,128)(2,1)S(1)}, bf16[256,2048]{1,0:T(8,128)(2,1)}, u32[]{:S(2)}) copy-start(bf16[256,2048]{1,0:T(8,128)(2,1)} %q_ref.1) | copy-start | bytes 3145732
  1.9 0.9 %copy-start.1 = (bf16[256,256]{1,0:T(8,128)(2,1)S(1)}, bf16[256,256]{1,0:T(8,128)(2,1)}, u32[]{:S(2)}) copy-start(bf16[256,256]{1,0:T(8,128)(2,1)} %k_ref.1) | copy-start | bytes 393220
  2.8 0.9 %copy-start.2 = (bf16[256,256]{1,0:T(8,128)(2,1)S(1)}, bf16[256,256]{1,0:T(8,128)(2,1)}, u32[]{:S(2)}) copy-start(bf16[256,256]{1,0:T(8,128)(2,1)} %v_ref.1) | copy-start | bytes 393220

commit v2 on v1

v2 whole, which is shorter than its diff:
```python
import functools
import math

import jax
import jax.numpy as jnp
from jax import lax
from jax.experimental import pallas as pl
from jax.experimental.pallas import tpu as pltpu
from jax.sharding import PartitionSpec as P

HEAD_DIM = 128
HALF = 128
SECOND_DOC = 192
MASKED = -1e30
EXPONENT = math.log2(math.e) / math.sqrt(HEAD_DIM)
MESH = pl.DeviceIdType.MESH


def first_key_block(tile, doc0):
    later = jnp.where(tile < (doc0 + SECOND_DOC) // HALF + 1, doc0 // HALF, (doc0 + SECOND_DOC) // HALF)
    return jnp.where(tile < doc0 // HALF, 0, later)


def kernel(
    n, doc0, has_before, q_hbm, k_hbm, v_hbm, seg_hbm, *refs
):
    before_ref = refs[0] if has_before else None
    (
        out_ref, q_ref, k_ref, seg_ref, k_all, v_all, q_rot, acc, top, total,
        cos_ref, sin_ref, start_ref, v_turned, weights, shrink, send_sem, recv_sem, own_sem,
    ) = refs[has_before:]
    me = lax.axis_index("seq")
    rows = k_hbm.shape[0]
    halves = rows // HALF
    kv_heads = k_hbm.shape[1] // HEAD_DIM
    group = q_hbm.shape[1] // k_hbm.shape[1]
    first_row = me * rows

    own = [
        pltpu.make_async_copy(source, target, own_sem.at[place])
        for place, (source, target) in enumerate(
            ((seg_hbm, seg_ref), (k_hbm, k_ref), (q_hbm, q_ref), (v_hbm, v_all.at[me]))
        )
    ]
    for copy in own:
        copy.start()

    barrier = pltpu.get_barrier_semaphore()

    def first_source(device):
        low = first_key_block(device * halves, doc0)
        for half in range(1, halves):
            low = jnp.minimum(low, first_key_block(device * halves + half, doc0))
        return low // halves

    def passed_on(source):
        return (me + 1 < n) & (source >= first_source(me + 1))

    def receives():
        return first_source(me) < me

    def send(step, kind):
        source = me - step
        held = (v_all if kind else k_all).at[source]
        return pltpu.make_async_remote_copy(
            src_ref=v_hbm if kind and isinstance(step, int) else held,
            dst_ref=held,
            send_sem=send_sem.at[step + 1, kind],
            recv_sem=recv_sem.at[step + 1, kind],
            device_id={"seq": lax.rem(me + 1, n)},
            device_id_type=MESH,
        )

    @pl.when(receives())
    def _():
        pl.semaphore_signal(
            barrier, inc=1, device_id={"seq": lax.rem(me - 1 + n, n)}, device_id_type=MESH
        )

    @pl.when(passed_on(me))
    def _():
        pl.semaphore_wait(barrier, 1)
        send(0, 1).start()

    own[0].wait()
    seg_row = jnp.broadcast_to(seg_ref[...], (rows, rows))
    seg_column = seg_row.T

    def document_start(token, earlier, axis):
        count = jnp.sum(earlier.astype(jnp.float32), axis=axis, keepdims=True).astype(jnp.int32)
        start = first_row + count
        if has_before:
            start = jnp.where(count == 0, before_ref[0, 0], start)
        return jnp.where(token < doc0, 0, jnp.where(token < doc0 + SECOND_DOC, doc0, start))

    token = first_row + lax.broadcasted_iota(jnp.int32, (1, rows), 1)
    start_ref[...] = document_start(token, seg_column < seg_row, 0)
    token = first_row + lax.broadcasted_iota(jnp.int32, (rows, 1), 0)
    start = document_start(token, seg_row < seg_column, 1)
    lane = lax.broadcasted_iota(jnp.int32, (1, HEAD_DIM), 1)
    index = (lane % (HEAD_DIM // 2)).astype(jnp.float32)
    frequency = jnp.exp(index * (-math.log(1000000.0) / (HEAD_DIM // 2)))
    angles = (token - start).astype(jnp.float32) * frequency
    cos_ref[...] = jnp.cos(angles)
    sin_ref[...] = jnp.where(lane < HEAD_DIM // 2, -1.0, 1.0) * jnp.sin(angles)

    def turn(x, cos_part, sin_part):
        wide = x.astype(jnp.float32)
        swapped = pltpu.roll(wide, HEAD_DIM // 2, 1)
        return (wide * cos_part + swapped * sin_part).astype(jnp.bfloat16)

    own[1].wait()
    for head in range(kv_heads):
        columns = slice(head * HEAD_DIM, (head + 1) * HEAD_DIM)
        k_all[me, :, columns] = turn(k_ref[:, columns], cos_ref[...], sin_ref[...])
    @pl.when(passed_on(me))
    def _():
        send(0, 0).start()

    own[2].wait()
    for half in range(halves):
        part = slice(half * HALF, (half + 1) * HALF)
        for head in range(kv_heads * group):
            columns = slice(head * HEAD_DIM, (head + 1) * HEAD_DIM)
            q_rot[half, head // 2, head % 2 * HALF : (head % 2 + 1) * HALF] = turn(
                q_ref[part, columns], cos_ref[part], sin_ref[part]
            )

    pairs = kv_heads * group // 2
    columns_of = [
        slice(2 * pair // group * HEAD_DIM, (2 * pair // group + 1) * HEAD_DIM)
        for pair in range(pairs)
    ]

    def mask(half, source, upto):
        part = slice(half * HALF, (half + 1) * HALF)
        key = source * rows + lax.broadcasted_iota(jnp.int32, (upto, 1), 0)
        query = first_row + half * HALF + lax.broadcasted_iota(jnp.int32, (1, HALF), 1)
        allowed = (key >= start_ref[:, part]) & (key <= query)
        return jnp.concatenate([allowed, allowed], axis=1)

    def weigh(half, source, upto, first, allowed=None):
        for pair in range(pairs):
            found = lax.dot_general(
                k_all[source, :upto, columns_of[pair]],
                q_rot[half, pair],
                (((1,), (1,)), ((), ())),
                preferred_element_type=jnp.float32,
            )
            if allowed is not None:
                found = jnp.where(allowed, found, MASKED)
            peak = jnp.max(found, axis=0, keepdims=True)
            if not first:
                old = top[half, pair]
                peak = jnp.maximum(old, peak)
            weight = jnp.exp2((found - peak) * EXPONENT)
            part = jnp.sum(weight, axis=0, keepdims=True)
            if not first:
                factor = jnp.exp2((old - peak) * EXPONENT)
                shrink[half, pair] = factor
                part += total[half, pair] * factor
            top[half, pair] = peak
            total[half, pair] = part
            weights[half, pair, :upto] = weight.astype(jnp.bfloat16)

    def mix(half, upto, first):
        for pair in range(pairs):
            part = jnp.dot(
                v_turned[columns_of[pair], :upto],
                weights[half, pair, :upto],
                preferred_element_type=jnp.float32,
            )
            acc[half, pair] = part if first else acc[half, pair] * shrink[half, pair] + part

    def finish(half):
        part = slice(half * HALF, (half + 1) * HALF)
        for pair in range(pairs):
            found = (acc[half, pair] * (1.0 / total[half, pair])).astype(jnp.bfloat16).T
            for side in range(2):
                head = 2 * pair + side
                columns = slice(head * HEAD_DIM, (head + 1) * HEAD_DIM)
                out_ref[part, columns] = found[side * HALF : (side + 1) * HALF]

    lows = [first_key_block(me * halves + half, doc0) for half in range(halves)]

    for half in range(halves):
        weigh(half, me, (half + 1) * HALF, True, mask(half, me, (half + 1) * HALF))
    own[3].wait()
    v_turned[...] = v_all[me].T
    for half in range(halves):
        mix(half, (half + 1) * HALF, True)

        @pl.when(lows[half] >= me * halves)
        def _():
            finish(half)

    def absorb(step, carry):
        source = me - step

        def arrived(kind, ref):
            return pltpu.make_async_remote_copy(
                src_ref=ref.at[source],
                dst_ref=ref.at[source],
                send_sem=send_sem.at[step, kind],
                recv_sem=recv_sem.at[step, kind],
                device_id={"seq": lax.rem(me + 1, n)},
                device_id_type=MESH,
            )

        arrived(0, k_all).wait_recv()

        @pl.when(passed_on(source))
        def _():
            send(step, 0).start()
            arrived(1, v_all).wait_recv()
            send(step, 1).start()

        for half in range(halves):
            seen = (source + 1) * halves > lows[half]
            inside = me * halves + half < doc0 // HALF

            @pl.when(seen & inside)
            def _():
                weigh(half, source, rows, False)

            @pl.when(seen & jnp.logical_not(inside))
            def _():
                weigh(half, source, rows, False, mask(half, source, rows))

        @pl.when(jnp.logical_not(passed_on(source)))
        def _():
            arrived(1, v_all).wait_recv()

        v_turned[...] = v_all[source].T
        for half in range(halves):
            @pl.when((source + 1) * halves > lows[half])
            def _():
                mix(half, rows, False)

        return carry

    lax.fori_loop(1, me - first_source(me) + 1, absorb, 0)

    for half in range(halves):
        @pl.when(lows[half] < me * halves)
        def _():
            finish(half)

    @pl.when(passed_on(me))
    def _():
        send(0, 1).wait_send()
        send(0, 0).wait_send()

    def sent(step, carry):
        @pl.when(passed_on(me - step))
        def _():
            send(step, 0).wait_send()
            send(step, 1).wait_send()

        return carry

    lax.fori_loop(1, me - first_source(me) + 1, sent, 0)


def shards(n, queries, keys, values, segments):
    rows = queries.shape[0]
    tokens = n * rows
    doc0 = tokens // 2 + HALF
    kv_heads = keys.shape[1] // HEAD_DIM
    heads = queries.shape[1] // HEAD_DIM
    halves = rows // HALF
    operands = [
        pltpu.with_memory_space_constraint(operand, pltpu.HBM)
        for operand in (queries, keys, values, segments.reshape(1, rows))
    ]
    specs = [pl.BlockSpec(memory_space=pltpu.HBM)] * 4
    has_before = (doc0 + SECOND_DOC) // rows < n - 1
    if has_before:
        every = lax.all_gather(segments, "seq", axis=0, tiled=True)
        before = jnp.sum((every < segments[0]).astype(jnp.int32))
        operands.append(before.reshape(1, 1))
        specs.append(pl.BlockSpec(memory_space=pltpu.SMEM))
    return pl.pallas_call(
        functools.partial(kernel, n, doc0, has_before),
        out_shape=jax.ShapeDtypeStruct(queries.shape, jnp.bfloat16),
        in_specs=specs,
        out_specs=pl.BlockSpec(memory_space=pltpu.VMEM),
        scratch_shapes=[
            pltpu.VMEM(queries.shape, jnp.bfloat16),
            pltpu.VMEM(keys.shape, jnp.bfloat16),
            pltpu.VMEM((1, rows), jnp.int32),
            pltpu.VMEM((n, rows, kv_heads * HEAD_DIM), jnp.bfloat16),
            pltpu.VMEM((n, rows, kv_heads * HEAD_DIM), jnp.bfloat16),
            pltpu.VMEM((halves, heads // 2, 2 * HALF, HEAD_DIM), jnp.bfloat16),
            pltpu.VMEM((halves, heads // 2, HEAD_DIM, 2 * HALF), jnp.float32),
            pltpu.VMEM((halves, heads // 2, 1, 2 * HALF), jnp.float32),
            pltpu.VMEM((halves, heads // 2, 1, 2 * HALF), jnp.float32),
            pltpu.VMEM((rows, HEAD_DIM), jnp.float32),
            pltpu.VMEM((rows, HEAD_DIM), jnp.float32),
            pltpu.VMEM((1, rows), jnp.int32),
            pltpu.VMEM((kv_heads * HEAD_DIM, rows), jnp.bfloat16),
            pltpu.VMEM((halves, heads // 2, rows, 2 * HALF), jnp.bfloat16),
            pltpu.VMEM((halves, heads // 2, 1, 2 * HALF), jnp.float32),
            pltpu.SemaphoreType.DMA((n + 1, 2)),
            pltpu.SemaphoreType.DMA((n + 1, 2)),
            pltpu.SemaphoreType.DMA((4,)),
        ],
        compiler_params=pltpu.CompilerParams(
            collective_id=0, has_side_effects=True, vmem_limit_bytes=48 * 1024 * 1024
        ),
    )(*operands)


def solution(mesh):
    placed = (
        P(("rep", "seq"), "tp"),
        P(("rep", "seq"), "tp"),
        P(("rep", "seq"), "tp"),
        P(("rep", "seq")),
    )
    return jax.shard_map(
        functools.partial(shards, mesh.shape["seq"]),
        mesh=mesh,
        in_specs=placed,
        out_specs=P(("rep", "seq"), "tp"),
        check_vma=False,
    )
```

time: 27.1 us -> 16.1 us (0.59)
  the two profiles are of different devices: /device:TPU:8 before, /device:TPU:16 now
where the time goes in v2:
time: 16.1 us; the launch traced here: 16 us
  Pallas kernels  15 us (93%)
  local copies, waits for them, and re-layouts  0.97 us (6%)
    pallas_call x1, Pallas kernels, shards(): pl.pallas_call(functools.partial(kernel, n, doc0, has_before), out_shape=...  15 us
    unnamed x1, local copies, waits for them, and re-layouts  0.97 us

profile of v2, /device:TPU:16, one launch (start us, length us, event | category | flops | bytes accessed | tf_op | source)
XLA Modules:
  0.0 16.0 jit_solution(16798664503089456005)
XLA Ops:
  0.0 15.0 %shard_map.46 = bf16[256,2048]{1,0:T(8,128)(2,1)S(1)} custom-call(bf16[256,2048]{1,0:T(8,128)(2,1)} %q_hbm.1, bf16[256,256]{1,0:T(8,128)(2,1)} %k_hbm.1, bf16[256,256]{1,0:T(8,128)(2,1)} %v_hbm.1, s32[1,256]{1,0:T(1,128)} %bitcast.1), custom_call_target="tpu_custom_call" | custom-call | tf_op jit(solution)/shard_map/pallas_call | solution.py:283
  15.0 1.0 %copy.6 = bf16[256,2048]{1,0:T(8,128)(2,1)} copy(bf16[256,2048]{1,0:T(8,128)(2,1)S(1)} %shard_map.46) | data formatting | bytes 2097152

commit v3 on v2

--- a/solution.py
+++ b/solution.py
@@ -36,15 +36,6 @@
     group = q_hbm.shape[1] // k_hbm.shape[1]
     first_row = me * rows
 
-    own = [
-        pltpu.make_async_copy(source, target, own_sem.at[place])
-        for place, (source, target) in enumerate(
-            ((seg_hbm, seg_ref), (k_hbm, k_ref), (q_hbm, q_ref), (v_hbm, v_all.at[me]))
-        )
-    ]
-    for copy in own:
-        copy.start()
-
     barrier = pltpu.get_barrier_semaphore()
 
     def first_source(device):
@@ -59,28 +50,53 @@
     def receives():
         return first_source(me) < me
 
-    def send(step, kind):
-        source = me - step
-        held = (v_all if kind else k_all).at[source]
-        return pltpu.make_async_remote_copy(
-            src_ref=v_hbm if kind and isinstance(step, int) else held,
-            dst_ref=held,
-            send_sem=send_sem.at[step + 1, kind],
-            recv_sem=recv_sem.at[step + 1, kind],
-            device_id={"seq": lax.rem(me + 1, n)},
-            device_id_type=MESH,
-        )
-
     @pl.when(receives())
     def _():
         pl.semaphore_signal(
             barrier, inc=1, device_id={"seq": lax.rem(me - 1 + n, n)}, device_id_type=MESH
         )
 
+    def head_columns(head):
+        return slice(head * HEAD_DIM, (head + 1) * HEAD_DIM)
+
+    own = [
+        pltpu.make_async_copy(source, target, own_sem.at[place])
+        for place, (source, target) in enumerate(
+            [(seg_hbm, seg_ref), (k_hbm, k_ref), (q_hbm, q_ref)]
+            + [(v_hbm.at[:, head_columns(kv)], v_all.at[me, kv]) for kv in range(kv_heads)]
+        )
+    ]
+    for copy in own[3:] + own[:3]:
+        copy.start()
+
+    def send(step, held, kind, kv):
+        return pltpu.make_async_remote_copy(
+            src_ref=held.at[me - step, kv],
+            dst_ref=held.at[me - step, kv],
+            send_sem=send_sem.at[step + 1, kind, kv],
+            recv_sem=recv_sem.at[step + 1, kind, kv],
+            device_id={"seq": lax.rem(me + 1, n)},
+            device_id_type=MESH,
+        )
+
+    def arrived(step, held, kind, kv):
+        return pltpu.make_async_remote_copy(
+            src_ref=held.at[me - step, kv],
+            dst_ref=held.at[me - step, kv],
+            send_sem=send_sem.at[step, kind, kv],
+            recv_sem=recv_sem.at[step, kind, kv],
+            device_id={"seq": lax.rem(me + 1, n)},
+            device_id_type=MESH,
+        )
+
+    for copy in own[3:]:
+        copy.wait()
+
     @pl.when(passed_on(me))
     def _():
         pl.semaphore_wait(barrier, 1)
-        send(0, 1).start()
+        for kv in range(kv_heads):
+            send(0, v_all, 1, kv).start()
 
     own[0].wait()
     seg_row = jnp.broadcast_to(seg_ref[...], (rows, rows))
@@ -110,12 +126,12 @@
         return (wide * cos_part + swapped * sin_part).astype(jnp.bfloat16)
 
     own[1].wait()
-    for head in range(kv_heads):
-        columns = slice(head * HEAD_DIM, (head + 1) * HEAD_DIM)
-        k_all[me, :, columns] = turn(k_ref[:, columns], cos_ref[...], sin_ref[...])
-    @pl.when(passed_on(me))
-    def _():
-        send(0, 0).start()
+    for kv in range(kv_heads):
+        k_all[me, kv] = turn(k_ref[:, head_columns(kv)], cos_ref[...], sin_ref[...])
+
+        @pl.when(passed_on(me))
+        def _():
+            send(0, k_all, 0, kv).start()
 
     own[2].wait()
     for half in range(halves):
@@ -127,10 +143,7 @@
             )
 
     pairs = kv_heads * group // 2
-    columns_of = [
-        slice(2 * pair // group * HEAD_DIM, (2 * pair // group + 1) * HEAD_DIM)
-        for pair in range(pairs)
-    ]
+    per_kv = group // 2
 
     def mask(half, source, upto):
         part = slice(half * HALF, (half + 1) * HALF)
@@ -142,7 +155,7 @@
     def weigh(half, source, upto, first, allowed=None):
         for pair in range(pairs):
             found = lax.dot_general(
-                k_all[source, :upto, columns_of[pair]],
+                k_all[source, pair // per_kv, :upto],
                 q_rot[half, pair],
                 (((1,), (1,)), ((), ())),
                 preferred_element_type=jnp.float32,
@@ -163,18 +176,18 @@
             total[half, pair] = part
             weights[half, pair, :upto] = weight.astype(jnp.bfloat16)
 
-    def mix(half, upto, first):
-        for pair in range(pairs):
+    def mix(half, kv, upto, first):
+        for pair in range(kv * per_kv, (kv + 1) * per_kv):
             part = jnp.dot(
-                v_turned[columns_of[pair], :upto],
+                v_turned[kv, :, :upto],
                 weights[half, pair, :upto],
                 preferred_element_type=jnp.float32,
             )
             acc[half, pair] = part if first else acc[half, pair] * shrink[half, pair] + part
 
-    def finish(half):
+    def finish(half, kv):
         part = slice(half * HALF, (half + 1) * HALF)
-        for pair in range(pairs):
+        for pair in range(kv * per_kv, (kv + 1) * per_kv):
             found = (acc[half, pair] * (1.0 / total[half, pair])).astype(jnp.bfloat16).T
             for side in range(2):
                 head = 2 * pair + side
@@ -185,35 +198,28 @@
 
     for half in range(halves):
         weigh(half, me, (half + 1) * HALF, True, mask(half, me, (half + 1) * HALF))
-    own[3].wait()
-    v_turned[...] = v_all[me].T
-    for half in range(halves):
-        mix(half, (half + 1) * HALF, True)
-
-        @pl.when(lows[half] >= me * halves)
-        def _():
-            finish(half)
+    for kv in range(kv_heads):
+        v_turned[kv] = v_all[me, kv].T
+        for half in range(halves):
+            mix(half, kv, (half + 1) * HALF, True)
+
+            @pl.when(lows[half] >= me * halves)
+            def _():
+                finish(half, kv)
 
     def absorb(step, carry):
         source = me - step
 
-        def arrived(kind, ref):
-            return pltpu.make_async_remote_copy(
-                src_ref=ref.at[source],
-                dst_ref=ref.at[source],
-                send_sem=send_sem.at[step, kind],
-                recv_sem=recv_sem.at[step, kind],
-                device_id={"seq": lax.rem(me + 1, n)},
-                device_id_type=MESH,
-            )
-
-        arrived(0, k_all).wait_recv()
+        for kv in range(kv_heads):
+            arrived(step, k_all, 0, kv).wait_recv()
 
         @pl.when(passed_on(source))
         def _():
-            send(step, 0).start()
-            arrived(1, v_all).wait_recv()
-            send(step, 1).start()
+            for kv in range(kv_heads):
+                send(step, k_all, 0, kv).start()
+            for kv in range(kv_heads):
+                arrived(step, v_all, 1, kv).wait_recv()
+                send(step, v_all, 1, kv).start()
 
         for half in range(halves):
             seen = (source + 1) * halves > lows[half]
@@ -227,35 +233,39 @@
             def _():
                 weigh(half, source, rows, False, mask(half, source, rows))
 
-        @pl.when(jnp.logical_not(passed_on(source)))
-        def _():
-            arrived(1, v_all).wait_recv()
-
-        v_turned[...] = v_all[source].T
-        for half in range(halves):
-            @pl.when((source + 1) * halves > lows[half])
+        for kv in range(kv_heads):
+            @pl.when(jnp.logical_not(passed_on(source)))
             def _():
-                mix(half, rows, False)
+                arrived(step, v_all, 1, kv).wait_recv()
+
+            v_turned[kv] = v_all[source, kv].T
+            for half in range(halves):
+                @pl.when((source + 1) * halves > lows[half])
+                def _():
+                    mix(half, kv, rows, False)
+
+                last = lows[half] // halves == source
+
+                @pl.when(last)
+                def _():
+                    finish(half, kv)
 
         return carry
 
     lax.fori_loop(1, me - first_source(me) + 1, absorb, 0)
-
-    for half in range(halves):
-        @pl.when(lows[half] < me * halves)
-        def _():
-            finish(half)
 
     @pl.when(passed_on(me))
     def _():
-        send(0, 1).wait_send()
-        send(0, 0).wait_send()
+        for kv in range(kv_heads):
+            send(0, v_all, 1, kv).wait_send()
+            send(0, k_all, 0, kv).wait_send()
 
     def sent(step, carry):
         @pl.when(passed_on(me - step))
         def _():
-            send(step, 0).wait_send()
-            send(step, 1).wait_send()
+            for kv in range(kv_heads):
+                send(step, k_all, 0, kv).wait_send()
+                send(step, v_all, 1, kv).wait_send()
 
         return carry
 
@@ -289,8 +299,8 @@
             pltpu.VMEM(queries.shape, jnp.bfloat16),
             pltpu.VMEM(keys.shape, jnp.bfloat16),
             pltpu.VMEM((1, rows), jnp.int32),
-            pltpu.VMEM((n, rows, kv_heads * HEAD_DIM), jnp.bfloat16),
-            pltpu.VMEM((n, rows, kv_heads * HEAD_DIM), jnp.bfloat16),
+            pltpu.VMEM((n, kv_heads, rows, HEAD_DIM), jnp.bfloat16),
+            pltpu.VMEM((n, kv_heads, rows, HEAD_DIM), jnp.bfloat16),
             pltpu.VMEM((halves, heads // 2, 2 * HALF, HEAD_DIM), jnp.bfloat16),
             pltpu.VMEM((halves, heads // 2, HEAD_DIM, 2 * HALF), jnp.float32),
             pltpu.VMEM((halves, heads // 2, 1, 2 * HALF), jnp.float32),
@@ -298,12 +308,12 @@
             pltpu.VMEM((rows, HEAD_DIM), jnp.float32),
             pltpu.VMEM((rows, HEAD_DIM), jnp.float32),
             pltpu.VMEM((1, rows), jnp.int32),
-            pltpu.VMEM((kv_heads * HEAD_DIM, rows), jnp.bfloat16),
+            pltpu.VMEM((kv_heads, HEAD_DIM, rows), jnp.bfloat16),
             pltpu.VMEM((halves, heads // 2, rows, 2 * HALF), jnp.bfloat16),
             pltpu.VMEM((halves, heads // 2, 1, 2 * HALF), jnp.float32),
-            pltpu.SemaphoreType.DMA((n + 1, 2)),
-            pltpu.SemaphoreType.DMA((n + 1, 2)),
-            pltpu.SemaphoreType.DMA((4,)),
+            pltpu.SemaphoreType.DMA((n + 1, 2, kv_heads)),
+            pltpu.SemaphoreType.DMA((n + 1, 2, kv_heads)),
+            pltpu.SemaphoreType.DMA((3 + kv_heads,)),
         ],
         compiler_params=pltpu.CompilerParams(
             collective_id=0, has_side_effects=True, vmem_limit_bytes=48 * 1024 * 1024

time: 16.1 us -> 15.9 us (0.988)
  Pallas kernels: 15 us -> 14.8 us
    pallas_call x1, Pallas kernels: 15 us -> 14.8 us  [shards(): pl.pallas_call(functools.partial(kernel, n, doc0, has_before), out_shape=...]
where the time goes in v3:
time: 15.9 us; the launch traced here: 15.8 us
  Pallas kernels  14.8 us (93%)
  local copies, waits for them, and re-layouts  0.97 us (6%)
    pallas_call x1, Pallas kernels, shards(): pl.pallas_call(functools.partial(kernel, n, doc0, has_before), out_shape=...  14.8 us
    unnamed x1, local copies, waits for them, and re-layouts  0.97 us

profile of v3, /device:TPU:16, one launch (start us, length us, event | category | flops | bytes accessed | tf_op | source)
XLA Modules:
  0.0 15.8 jit_solution(16759199025484847916)
XLA Ops:
  0.0 14.8 %shard_map.46 = bf16[256,2048]{1,0:T(8,128)(2,1)S(1)} custom-call(bf16[256,2048]{1,0:T(8,128)(2,1)} %q_hbm.1, bf16[256,256]{1,0:T(8,128)(2,1)} %k_hbm.1, bf16[256,256]{1,0:T(8,128)(2,1)} %v_hbm.1, s32[1,256]{1,0:T(1,128)} %bitcast.1), custom_call_target="tpu_custom_call" | custom-call | tf_op jit(solution)/shard_map/pallas_call | solution.py:293
  14.8 1.0 %copy.6 = bf16[256,2048]{1,0:T(8,128)(2,1)} copy(bf16[256,2048]{1,0:T(8,128)(2,1)S(1)} %shard_map.46) | data formatting | bytes 2097152

commit v4 on v3

--- a/solution.py
+++ b/solution.py
@@ -50,12 +50,6 @@
     def receives():
         return first_source(me) < me
 
-    @pl.when(receives())
-    def _():
-        pl.semaphore_signal(
-            barrier, inc=1, device_id={"seq": lax.rem(me - 1 + n, n)}, device_id_type=MESH
-        )
-
     def head_columns(head):
         return slice(head * HEAD_DIM, (head + 1) * HEAD_DIM)
 
@@ -66,29 +60,36 @@
             + [(v_hbm.at[:, head_columns(kv)], v_all.at[me, kv]) for kv in range(kv_heads)]
         )
     ]
-    for copy in own[3:] + own[:3]:
+    for copy in own[3:] + own[:2]:
         copy.start()
+
+    @pl.when(receives())
+    def _():
+        pl.semaphore_signal(
+            barrier, inc=1, device_id={"seq": lax.rem(me - 1 + n, n)}, device_id_type=MESH
+        )
 
     def send(step, held, kind, kv):
         return pltpu.make_async_remote_copy(
-            src_ref=held.at[me - step, kv],
-            dst_ref=held.at[me - step, kv],
-            send_sem=send_sem.at[step + 1, kind, kv],
-            recv_sem=recv_sem.at[step + 1, kind, kv],
+            src_ref=held.at[me - step] if kv is None else held.at[me - step, kv],
+            dst_ref=held.at[me - step] if kv is None else held.at[me - step, kv],
+            send_sem=send_sem.at[step + 1, kind, kv or 0],
+            recv_sem=recv_sem.at[step + 1, kind, kv or 0],
             device_id={"seq": lax.rem(me + 1, n)},
             device_id_type=MESH,
         )
 
     def arrived(step, held, kind, kv):
         return pltpu.make_async_remote_copy(
-            src_ref=held.at[me - step, kv],
-            dst_ref=held.at[me - step, kv],
-            send_sem=send_sem.at[step, kind, kv],
-            recv_sem=recv_sem.at[step, kind, kv],
+            src_ref=held.at[me - step] if kv is None else held.at[me - step, kv],
+            dst_ref=held.at[me - step] if kv is None else held.at[me - step, kv],
+            send_sem=send_sem.at[step, kind, kv or 0],
+            recv_sem=recv_sem.at[step, kind, kv or 0],
             device_id={"seq": lax.rem(me + 1, n)},
             device_id_type=MESH,
         )
 
+    own[2].start()
     for copy in own[3:]:
         copy.wait()
 
@@ -129,9 +130,9 @@
     for kv in range(kv_heads):
         k_all[me, kv] = turn(k_ref[:, head_columns(kv)], cos_ref[...], sin_ref[...])
 
-        @pl.when(passed_on(me))
-        def _():
-            send(0, k_all, 0, kv).start()
+    @pl.when(passed_on(me))
+    def _():
+        send(0, k_all, 0, None).start()
 
     own[2].wait()
     for half in range(halves):
@@ -210,13 +211,11 @@
     def absorb(step, carry):
         source = me - step
 
-        for kv in range(kv_heads):
-            arrived(step, k_all, 0, kv).wait_recv()
+        arrived(step, k_all, 0, None).wait_recv()
 
         @pl.when(passed_on(source))
         def _():
-            for kv in range(kv_heads):
-                send(step, k_all, 0, kv).start()
+            send(step, k_all, 0, None).start()
             for kv in range(kv_heads):
                 arrived(step, v_all, 1, kv).wait_recv()
                 send(step, v_all, 1, kv).start()
@@ -258,13 +257,13 @@
     def _():
         for kv in range(kv_heads):
             send(0, v_all, 1, kv).wait_send()
-            send(0, k_all, 0, kv).wait_send()
+        send(0, k_all, 0, None).wait_send()
 
     def sent(step, carry):
         @pl.when(passed_on(me - step))
         def _():
+            send(step, k_all, 0, None).wait_send()
             for kv in range(kv_heads):
-                send(step, k_all, 0, kv).wait_send()
                 send(step, v_all, 1, kv).wait_send()
 
         return carry

time: 15.9 us -> 15.9 us (level)
  no operation moved by 1% of the time
where the time goes in v4:
time: 15.9 us; the launch traced here: 15.8 us
  Pallas kernels  14.8 us (93%)
  local copies, waits for them, and re-layouts  0.97 us (6%)
    pallas_call x1, Pallas kernels, shards(): pl.pallas_call(functools.partial(kernel, n, doc0, has_before), out_shape=...  14.8 us
    unnamed x1, local copies, waits for them, and re-layouts  0.97 us

profile of v4, /device:TPU:16, one launch (start us, length us, event | category | flops | bytes accessed | tf_op | source)
XLA Modules:
  0.0 15.8 jit_solution(3155823614150124856)
XLA Ops:
  0.0 14.8 %shard_map.46 = bf16[256,2048]{1,0:T(8,128)(2,1)S(1)} custom-call(bf16[256,2048]{1,0:T(8,128)(2,1)} %q_hbm.1, bf16[256,256]{1,0:T(8,128)(2,1)} %k_hbm.1, bf16[256,256]{1,0:T(8,128)(2,1)} %v_hbm.1, s32[1,256]{1,0:T(1,128)} %bitcast.1), custom_call_target="tpu_custom_call" | custom-call | tf_op jit(solution)/shard_map/pallas_call | solution.py:292
  14.8 1.0 %copy.6 = bf16[256,2048]{1,0:T(8,128)(2,1)} copy(bf16[256,2048]{1,0:T(8,128)(2,1)S(1)} %shard_map.46) | data formatting | bytes 2097152
